TPU v7x, 32 devices: a whole 2x2x4 slice. The times are simulated.
32 devices in a mesh: band: 4 (over y, core), tile: 8 (over z, x).
Axes of the slice: x: 2, y: 2, z: 4, core: 2. Of those that a mesh axis runs over, the one named last changes fastest.
Arguments:
- traces: float32 [64, 64, 1024], P(None, ('band', 'tile')), may hold values from -6 to 6
- bins: int32 [8], replicated, may hold values from 1 to 31, as said below
Outputs:
- dip_fields: float32 [8, 2, 64, 64, 128], P('band', None, 'tile')
Inputs may be any that keep to these rules, and one draw needn't show every extreme that they name: 8 distinct bins, 1 and 31 among them.
All inputs are finite; a program needn't handle non-finite values.
Results may differ from a plain program's by a relative error of at most 0.00018.
Values sent between devices are 32-bit elements; how exact they have to be, the bound alone decides.
No kernel may reach another device: no remote copies, remote signals or barrier semaphores. Data moves between devices by JAX's collectives and lax.ppermute only.
A program may use at most 128 MiB of HBM per device.

v0:
```python
import math

import jax
import jax.numpy as jnp
from jax import lax
from jax.sharding import PartitionSpec as P

NT = 1024
NB = 8
WIN = 64
HOP = 8
SEG = 128
R = 3
NF = 128


smooth_sigma = 2.0
tiny_value = 1e-06


def extended_2(block, sides, width):
    for axis, dim in sides:
        count = lax.axis_size(axis)
        forward = [(i, i + 1) for i in range(count - 1)]
        backward = [(target, source) for source, target in forward]
        low = lax.ppermute(
            lax.slice_in_dim(block, block.shape[dim] - width, None, axis=dim), axis, forward
        )
        high = lax.ppermute(lax.slice_in_dim(block, 0, width, axis=dim), axis, backward)
        block = jnp.concatenate([low, block, high], axis=dim)
    return block


def window_kernel(bins):
    band_count = bins.shape[0]
    sample_index = jnp.arange(WIN, dtype=jnp.int32)
    window_taper = 0.5 - 0.5 * jnp.cos(2.0 * math.pi / WIN * sample_index.astype(jnp.float32))
    phase_turns = bins[:, None] * sample_index[None, :] % WIN
    angles = 2.0 * math.pi / WIN * phase_turns.astype(jnp.float32)
    basis_rows = jnp.stack([window_taper * jnp.cos(angles), -window_taper * jnp.sin(angles)])
    frame_count = SEG // HOP
    seg_span = SEG + WIN - HOP
    offset = (
        jnp.arange(seg_span, dtype=jnp.int32)[:, None]
        - HOP * jnp.arange(frame_count, dtype=jnp.int32)[None, :]
    )
    inside = (offset >= 0) & (offset < WIN)
    picked = jnp.take(basis_rows, jnp.clip(offset, 0, WIN - 1), axis=2)
    kernel_table = jnp.where(inside[None, None], picked, 0.0)
    return jnp.transpose(kernel_table, (2, 0, 1, 3)).reshape(seg_span, 2 * band_count * frame_count)


def band_amplitude(traces, dft_kernel):
    frame_count = SEG // HOP
    seg_span = SEG + WIN - HOP
    block_count = NT // SEG
    band_count = dft_kernel.shape[1] // (2 * frame_count)
    padded = jnp.pad(traces, ((0, 0), (0, 0), (WIN // 2, WIN // 2)))
    pieces = jnp.stack(
        [padded[:, :, block * SEG : block * SEG + seg_span] for block in range(block_count)], axis=2
    )
    spectra = jnp.dot(
        pieces, dft_kernel, precision=lax.Precision.HIGHEST, preferred_element_type=jnp.float32
    )
    spectra = spectra.reshape(
        traces.shape[0], traces.shape[1], block_count, 2, band_count, frame_count
    )
    real_part = spectra[:, :, :, 0]
    imag_part = spectra[:, :, :, 1]
    return jnp.sqrt(real_part * real_part + imag_part * imag_part)


def gradients(padded):
    grad_il = (padded[2:, 1:-1, 1:-1] - padded[:-2, 1:-1, 1:-1]) * 0.5
    grad_xl = (padded[1:-1, 2:, 1:-1] - padded[1:-1, :-2, 1:-1]) * 0.5
    grad_time = (padded[1:-1, 1:-1, 2:] - padded[1:-1, 1:-1, :-2]) * 0.5
    return (grad_il, grad_xl, grad_time)


def smooth_axis(field, axis, length):
    weights = [
        math.exp(-(offset_step * offset_step) / (2.0 * smooth_sigma * smooth_sigma))
        for offset_step in range(-R, R + 1)
    ]
    weight_sum = sum(weights)
    result = None
    for position, weight in enumerate(weights):
        section = lax.slice_in_dim(field, position, position + length, axis=axis)
        scaled = weight / weight_sum * section
        result = scaled if result is None else result + scaled
    return result


def smoothed_dips(grad_il, grad_xl, grad_time):
    width = grad_il.shape[0] - 2 * R
    stacked = jnp.stack([grad_il * grad_time, grad_xl * grad_time, grad_time * grad_time])
    along_rows = smooth_axis(stacked, 1, width)
    cross_pad = jnp.pad(along_rows, ((0, 0), (0, 0), (R, R), (0, 0)))
    along_cross = smooth_axis(cross_pad, 2, along_rows.shape[2])
    time_pad = jnp.pad(along_cross, ((0, 0), (0, 0), (0, 0), (R, R)))
    tensor = smooth_axis(time_pad, 3, along_rows.shape[3])
    denominator = tensor[2] + tiny_value
    return jnp.stack([-tensor[0] / denominator, -tensor[1] / denominator])


def local(traces, bins):
    dft_kernel = window_kernel(bins)
    amplitude = band_amplitude(traces, dft_kernel)
    n_band = lax.axis_size("band")
    n_tile = lax.axis_size("tile")
    device_count = n_band * n_tile
    il_all = traces.shape[0]
    xl_part = traces.shape[1]
    tile_rows = il_all // n_tile
    band_group = NB // n_band
    frame_count = SEG // HOP
    block_count = NT // SEG
    rim_width = R + 1
    spectrum = amplitude.reshape(il_all, xl_part, block_count, n_band, band_group, frame_count)
    by_tile = spectrum.reshape(
        n_tile, tile_rows, xl_part, block_count, n_band, band_group, frame_count
    )
    payload = jnp.transpose(by_tile, (4, 0, 5, 1, 2, 3, 6))
    payload = payload.reshape(n_band, n_tile, band_group, tile_rows, xl_part, NF)
    outgoing = payload.reshape(device_count, band_group, tile_rows, xl_part, NF)
    bricks = lax.all_to_all(outgoing, ("band", "tile"), split_axis=0, concat_axis=3, tiled=True)
    bricks = bricks.reshape(band_group, tile_rows, device_count * xl_part, NF)
    bricks = extended_2(bricks, (("tile", 1),), rim_width)
    global_row = (
        lax.axis_index("tile") * tile_rows - R + jnp.arange(tile_rows + 2 * R, dtype=jnp.int32)
    )
    inside_mask = ((global_row >= 0) & (global_row < tile_rows * n_tile)).astype(jnp.float32)[
        :, None, None
    ]

    def brick_dips(extended):
        grad_il, grad_xl, grad_time = gradients(jnp.pad(extended, ((0, 0), (1, 1), (1, 1))))
        return smoothed_dips(grad_il * inside_mask, grad_xl * inside_mask, grad_time * inside_mask)

    return lax.map(brick_dips, bricks)


def solution(mesh):
    in_specs = (P(None, ("band", "tile"), None), P())
    out_specs = P("band", None, "tile", None, None)
    return jax.shard_map(local, mesh=mesh, in_specs=in_specs, out_specs=out_specs, check_vma=False)
```

profile of v0, /device:TPU:0, one launch (start us, length us, event | category | flops | bytes accessed | tf_op | source)
XLA Modules:
  0.0 86.1 jit_solution(9120787879538369387)
XLA Ops:
  0.2 2.7 %pad_slice_fusion.16 = (f32[64,2,184]{2,1,0:T(2,128)S(1)}, f32[64,2,184]{2,1,0:T(2,128)S(1)}, f32[64,2,184]{2,1,0:T(2,128)S(1)}, f32[64,2,184]{2,1,0:T(2,128)S(1...) fusion(f32[64,2,1024]{2,1,0:T(2,128)} %param.4), kind=kLoop, calls=%fused_computation.88 | loop fusion | bytes 2064384 | tf_op jit(solution)/shard_map/slice | solution.py:60
  3.2 0.7 stack.67
  4.0 0.7 stack.68
  4.7 0.8 stack.69
  5.5 0.8 stack.70
  6.2 0.7 stack.71
  7.3 9.6 %gather_fusion = f32[2944,2,8]{2,1,0:T(2,128)S(1)} fusion(f32[2,8,64]{1,0,2:T(2,128)S(1)} %copy.23, s32[3072]{0:T(1024)S(1)} %pad_clamp_fusion), kind=kCustom, calls=%fused_computation | custom fusion | bytes 388608 | tf_op jit(solution)/shard_map/jit(_take)/gather | solution.py:48
  16.9 3.7 %copy.31 = f32[184,16,2,8]{1,0,3,2:T(8,128)} copy(f32[184,16,2,8]{3,2,1,0:T(2,128)S(1)} %bitcast.68) | data formatting | bytes 376832 | tf_op jit(solution)/shard_map/jit(_take)/gather | solution.py:48
  20.9 1.5 %select_bitcast_fusion = f32[184,2,8,16]{3,0,2,1:T(8,128)S(1)} fusion(f32[184,16,2,8]{1,0,3,2:T(8,128)} %copy.31, pred[184,16]{1,0:T(8,128)(4,1)S(1)} %copy.21, pred[184,16]{1,0:T(8,128)(4,1)S(1)} %copy.22), kind=kLoop, calls=%fused_computation.84 | loop fusion | flops 94208 | bytes 382720 | tf_op jit(solution)/shard_map/jit(_where)/select_n | solution.py:49
  23.6 1.6 %stack.72 = f32[64,2,8,184]{3,2,1,0:T(8,128)S(1)} concatenate(f32[64,2,1,184]{3,2,1,0:T(1,128)S(1)} %copy.20, f32[64,2,1,184]{3,2,1,0:T(1,128)S(1)} %stack.65, f32[64,2,1,184]{3,2,1,0:T(1,128)S(1)} %stack.66, f32[64,2,1,184]{3,2,1,0:T(1,128)S(1)} %copy-done, f32[64,2,1,184]{3,2,1,0:T(1,128)S(1)} %copy-done.1, f32[64,2,1,184]{3,2,1,0:T(1,128)S(1)} %copy-done.2, ...), dimensions={2} | concatenate | bytes 1507328 | tf_op jit(solution)/shard_map/stack | solution.py:59
  25.2 7.1 %fusion.48 = f32[64,2,8,2,8,16]{5,2,4,3,1,0:T(8,128)S(1)} fusion(f32[64,2,8,184]{3,2,1,0:T(8,128)S(1)} %stack.72, f32[184,2,8,16]{0,3,2,1:T(8,128)S(1)} %copy.25), kind=kOutput, calls=%fused_computation.86 | convolution fusion | flops 578813952 | bytes 1990656 | tf_op jit(solution)/shard_map/dot_general | solution.py:62
  32.4 1.6 %fusion.47 = f32[64,2,8,1,8,16]{5,2,4,3,1,0:T(8,128)S(1)} fusion(f32[64,2,8,2,8,16]{5,2,4,3,1,0:T(8,128)S(1)} %fusion.48), kind=kLoop, calls=%fused_computation.81 | loop fusion | flops 393216 | bytes 1572864 | tf_op jit(solution)/shard_map/sqrt | solution.py:70
  33.9 2.6 %copy.37 = f32[8,8,2,8,4,2,16]{6,3,1,2,5,0,4:T(8,128)} copy(f32[8,8,2,8,4,2,16]{6,3,5,4,2,1,0:T(8,128)S(1)} %bitcast.66) | data formatting | bytes 1048576 | tf_op jit(solution)/shard_map/sqrt | solution.py:70
  36.5 3.2 %reshape_reshape.4 = f32[32,2,8,2,128]{4,2,3,1,0:T(8,128)S(1)} reshape(f32[4,8,2,8,2,8,16]{6,5,3,4,2,1,0:T(8,128)} %bitcast.67) | data formatting | bytes 1048576 | tf_op jit(solution)/shard_map/reshape;reshape | solution.py:125
  39.7 23.5 %all_to_all.15 = f32[32,2,8,2,128]{4,2,3,1,0:T(8,128)S(1)} all-to-all(f32[32,2,8,2,128]{4,2,3,1,0:T(8,128)S(1)} %reshape_reshape.4), channel_id=1, replica_groups=mesh['band'=4,'tile'=8] {'band','tile'}, dimensions={0} | all-to-all | bytes 1048576 | tf_op jit(solution)/shard_map/all_to_all | solution.py:126
  63.3 2.8 %collective-permute-start = (f32[2,4,64,128]{3,1,2,0:T(4,128)S(1)}, f32[2,4,64,128]{3,1,2,0:T(4,128)S(1)}, u32[]{:S(2)}, u32[]{:S(2)}) collective-permute-start(f32[2,4,64,128]{3,1,2,0:T(4,128)S(1)} %get-tuple-element.97), channel_id=1, source_target_pairs={{0,1},{1,2},{2,3},{3,4},{4,5},{5,6},{6,7},{8,9},{9,10},{10,11},{11... | collective-permute-start | bytes 786440 | tf_op jit(solution)/shard_map/ppermute | solution.py:26
  66.1 1.3 %collective-permute-start.1 = (f32[2,4,64,128]{3,1,2,0:T(4,128)S(1)}, f32[2,4,64,128]{3,1,2,0:T(4,128)S(1)}, u32[]{:S(2)}, u32[]{:S(2)}) collective-permute-start(f32[2,4,64,128]{3,1,2,0:T(4,128)S(1)} %get-tuple-element.98), channel_id=1, source_target_pairs={{1,0},{2,1},{3,2},{4,3},{5,4},{6,5},{7,6},{9,8},{10,9},{11,10},{12... | collective-permute-start | bytes 786440 | tf_op jit(solution)/shard_map/ppermute | solution.py:29
  67.4 10.1 %collective-permute-done = f32[2,4,64,128]{3,1,2,0:T(4,128)S(1)} collective-permute-done((f32[2,4,64,128]{3,1,2,0:T(4,128)S(1)}, f32[2,4,64,128]{3,1,2,0:T(4,128)S(1)}, u32[]{:S(2)}, u32[]{:S(2)}) %collective-permute-start) | collective-permute-done | bytes 262176 | tf_op jit(solution)/shard_map/ppermute | solution.py:26
  77.7 7.4 %while.13 = (s32[]{:T(128)}, f32[2,2,8,64,128]{4,3,2,1,0:T(8,128)S(1)}, f32[2,16,64,128]{3,1,2,0:T(8,128)S(1)}, s32[]{:T(128)}, s32[]{:T(128)}) while((s32[]{:T(128)}, f32[2,2,8,64,128]{4,3,2,1,0:T(8,128)S(1)}, f32[2,16,64,128]{3,1,2,0:T(8,128)S(1)}, s32[]{:T(128)}, s32[]{:T(128)}) %tuple.53), condition=%wide.region_1.2_spmd.clone, body=%wide.region_0.1_spmd.clone.sunk | while | flops 10305608 | bytes 19464376 | solution.py:140
  78.1 0.9 %fusion.75 = (f32[1,14,64,128]{3,2,1,0:T(8,128)S(1)}, f32[1,14,64,128]{3,2,1,0:T(8,128)S(1)}, f32[1,14,64,128]{3,2,1,0:T(8,128)S(1)}) fusion(f32[1,16,64,128]{3,2,1,0:T(8,128)S(1)} %copy.39, f32[14]{0:T(128)S(1)} %fusion.74, f32[16,64,128]{2,1,0:T(8,128)S(1)} %bitcast.65), kind=kLoop, calls=%fused_computation.68.clone.1 | loop fusion | flops 1490944 | bytes 2818104 | tf_op jit(solution)/shard_map/while/body/eval_jaxpr/stack | solution.py:96
  80.1 1.3 %fusion.78 = f32[3,8,64,128]{3,2,1,0:T(8,128)S(1)} fusion(f32[3,8,64,128]{3,2,1,0:T(8,128)S(1)} %fusion.77), kind=kLoop, calls=%fused_computation.37.clone.1 | loop fusion | flops 2555904 | bytes 1572864 | tf_op jit(solution)/shard_map/while/body/eval_jaxpr/add | solution.py:90
  81.7 0.9 %fusion.75 = (f32[1,14,64,128]{3,2,1,0:T(8,128)S(1)}, f32[1,14,64,128]{3,2,1,0:T(8,128)S(1)}, f32[1,14,64,128]{3,2,1,0:T(8,128)S(1)}) fusion(f32[1,16,64,128]{3,2,1,0:T(8,128)S(1)} %copy.39, f32[14]{0:T(128)S(1)} %fusion.74, f32[16,64,128]{2,1,0:T(8,128)S(1)} %bitcast.65), kind=kLoop, calls=%fused_computation.68.clone.1 | loop fusion | flops 1490944 | bytes 2818104 | tf_op jit(solution)/shard_map/while/body/eval_jaxpr/stack | solution.py:96
  83.7 1.3 %fusion.78 = f32[3,8,64,128]{3,2,1,0:T(8,128)S(1)} fusion(f32[3,8,64,128]{3,2,1,0:T(8,128)S(1)} %fusion.77), kind=kLoop, calls=%fused_computation.37.clone.1 | loop fusion | flops 2555904 | bytes 1572864 | tf_op jit(solution)/shard_map/while/body/eval_jaxpr/add | solution.py:90
  85.1 1.0 %copy-done.6 = f32[2,2,8,64,128]{4,3,2,1,0:T(8,128)} copy-done((f32[2,2,8,64,128]{4,3,2,1,0:T(8,128)}, f32[2,2,8,64,128]{4,3,2,1,0:T(8,128)S(1)}, u32[]{:S(2)}) %copy-start.6) | copy-done | bytes 1048600
  (49 shorter events, 5.3 us)
Async XLA Ops:
  2.9 4.1 %copy-start.5 = (s32[8]{0:T(128)S(1)}, s32[8]{0:T(128)}, u32[]{:S(2)}) copy-start(s32[8]{0:T(128)} %param.5) | copy-start | bytes 100
  22.4 0.9 %copy-start = (f32[64,2,1,184]{3,2,1,0:T(1,128)S(1)}, f32[64,2,1,184]{3,2,1,0:T(1,128)}, u32[]{:S(2)}) copy-start(f32[64,2,1,184]{3,2,1,0:T(1,128)} %stack.67) | copy-start | bytes 282628
  22.4 1.0 %copy-start.1 = (f32[64,2,1,184]{3,2,1,0:T(1,128)S(1)}, f32[64,2,1,184]{3,2,1,0:T(1,128)}, u32[]{:S(2)}) copy-start(f32[64,2,1,184]{3,2,1,0:T(1,128)} %stack.68) | copy-start | bytes 282628
  22.4 1.0 %copy-start.2 = (f32[64,2,1,184]{3,2,1,0:T(1,128)S(1)}, f32[64,2,1,184]{3,2,1,0:T(1,128)}, u32[]{:S(2)}) copy-start(f32[64,2,1,184]{3,2,1,0:T(1,128)} %stack.69) | copy-start | bytes 282628
  22.4 1.1 %copy-start.3 = (f32[64,2,1,184]{3,2,1,0:T(1,128)S(1)}, f32[64,2,1,184]{3,2,1,0:T(1,128)}, u32[]{:S(2)}) copy-start(f32[64,2,1,184]{3,2,1,0:T(1,128)} %stack.70) | copy-start | bytes 282628
  22.5 1.1 %copy-start.4 = (f32[64,2,1,184]{3,2,1,0:T(1,128)S(1)}, f32[64,2,1,184]{3,2,1,0:T(1,128)}, u32[]{:S(2)}) copy-start(f32[64,2,1,184]{3,2,1,0:T(1,128)} %stack.71) | copy-start | bytes 282628
  63.3 14.2 %collective-permute-start = (f32[2,4,64,128]{3,1,2,0:T(4,128)S(1)}, f32[2,4,64,128]{3,1,2,0:T(4,128)S(1)}, u32[]{:S(2)}, u32[]{:S(2)}) collective-permute-start(f32[2,4,64,128]{3,1,2,0:T(4,128)S(1)} %get-tuple-element.97), channel_id=1, source_target_pairs={{0,1},{1,2},{2,3},{3,4},{4,5},{5,6},{6,7},{8,9},{9,10},{10,11},{11... | collective-permute-start | bytes 786440 | tf_op jit(solution)/shard_map/ppermute | solution.py:26
  66.1 11.4 %collective-permute-start.1 = (f32[2,4,64,128]{3,1,2,0:T(4,128)S(1)}, f32[2,4,64,128]{3,1,2,0:T(4,128)S(1)}, u32[]{:S(2)}, u32[]{:S(2)}) collective-permute-start(f32[2,4,64,128]{3,1,2,0:T(4,128)S(1)} %get-tuple-element.98), channel_id=1, source_target_pairs={{1,0},{2,1},{3,2},{4,3},{5,4},{6,5},{7,6},{9,8},{10,9},{11,10},{12... | collective-permute-start | bytes 786440 | tf_op jit(solution)/shard_map/ppermute | solution.py:29
  85.1 1.0 %copy-start.6 = (f32[2,2,8,64,128]{4,3,2,1,0:T(8,128)}, f32[2,2,8,64,128]{4,3,2,1,0:T(8,128)S(1)}, u32[]{:S(2)}) copy-start(f32[2,2,8,64,128]{4,3,2,1,0:T(8,128)S(1)} %get-tuple-element.169) | copy-start | bytes 3145732
where the time goes:
time: 86.7 us; the launch traced here: 86.1 us
  local copies, waits for them, and re-layouts  30.5 us (35%)
  blocking collectives  23.5 us (27%)
  other arithmetic  10.2 us (12%)
  waiting for transfers between devices  10.1 us (12%)
  matrix products  7.15 us (8%)
  starting transfers between devices  4.06 us (5%)
    all_to_all x1, blocking collectives, local(): lax.all_to_all(outgoing, ('band', 'tile'), split_axis=0, concat_axis=3, t...  23.5 us
    gather x2, local copies, waits for them, and re-layouts, window_kernel(): picked = jnp.take(basis_rows, jnp.clip(offset, 0, WIN - 1), axis=2)  13.3 us
    ppermute x1, waiting for transfers between devices, extended_2(): lax.ppermute(lax.slice_in_dim(block, block.shape[dim] - width, None, axis...  10.1 us
    dot_general x1, matrix products, band_amplitude(): jnp.dot(pieces, dft_kernel, precision=lax.Precision.HIGHEST, preferred_el...  7.15 us
    another operation x9, local copies, waits for them, and re-layouts, band_amplitude(): jnp.stack([padded[:, :, block * SEG:block * SEG + seg_span] for block in...  5.66 us
    add x6, other arithmetic, smooth_axis(): result = scaled if result is None else result + scaled  4.46 us
    another operation x1, local copies, waits for them, and re-layouts, local(): outgoing = payload.reshape(device_count, band_group, tile_rows, xl_part, NF)  3.24 us
    ppermute x1, starting transfers between devices, extended_2(): lax.ppermute(lax.slice_in_dim(block, block.shape[dim] - width, None, axis...  2.77 us
  transfers between devices with their start and end apart: 2, of which 1 were waited for; matrix products, arithmetic and copies ran while one was open for 0% of the time, Pallas kernels for 0%

commit v1 on v0

v1 whole, which is shorter than its diff:
```python
import math

import jax
import jax.numpy as jnp
from jax import lax
from jax.experimental import pallas as pl
from jax.experimental.pallas import tpu as pltpu
from jax.sharding import PartitionSpec as P

NT = 1024
NB = 8
WIN = 64
HOP = 8
SEG = 128
R = 3
NF = 128
SUB = 8
RIM = R + 1

smooth_sigma = 2.0
tiny_value = 1e-06

VMEM_LIMIT = 48 * 1024 * 1024


def stencil_weights():
    weights = [math.exp(-(k * k) / (2.0 * smooth_sigma * smooth_sigma)) for k in range(-R, R + 1)]
    return [weight / sum(weights) for weight in weights]


def turn_sine(turns):
    shifted = (turns + WIN // 4) & (WIN - 1)
    folded = (shifted & (WIN // 2 - 1)) - WIN // 4
    angle = folded.astype(jnp.float32) * (2.0 * math.pi / WIN)
    square = angle * angle
    series = jnp.full_like(angle, -1.0 / 39916800.0)
    for coefficient in (1.0 / 362880.0, -1.0 / 5040.0, 1.0 / 120.0, -1.0 / 6.0, 1.0):
        series = series * square + coefficient
    value = series * angle
    return jnp.where(shifted >= WIN // 2, -value, value)


def turn_cosine(turns):
    return turn_sine(turns + WIN // 4)


def split_halves(value):
    high = value.astype(jnp.bfloat16)
    low = (value - high.astype(jnp.float32)).astype(jnp.bfloat16)
    return high, low


def fill_table(bins_ref, table_ref):
    frames = SEG // HOP
    lane = lax.broadcasted_iota(jnp.int32, (SUB, SEG), 1)
    row = lax.broadcasted_iota(jnp.int32, (SUB, SEG), 0)
    frame, band = lane % frames, lane // frames
    bin_of = jnp.zeros((SUB, SEG), jnp.int32)
    for b in range(NB):
        bin_of = jnp.where(band == b, bins_ref[b], bin_of)
    cosines, sines = [], []
    for group in range(WIN // SUB):
        sample = row + group * SUB
        taper = 0.5 - 0.5 * turn_cosine(sample)
        turns = (bin_of * sample) & (WIN - 1)
        cosines.append(taper * turn_cosine(turns))
        sines.append(-taper * turn_sine(turns))
    zero = jnp.zeros((SUB, SEG), jnp.float32)
    front = WIN // 2 // SUB
    body = SEG // SUB
    tail = (WIN // 2 - HOP) // SUB
    for part, basis in enumerate((cosines, sines)):
        columns = pl.ds(part * SEG, SEG)
        for group in range(front + body + tail):
            value = zero
            for piece in range(WIN // SUB):
                if 0 <= group - piece < frames:
                    value = jnp.where(frame == group - piece, basis[piece], value)
            if group < front:
                at = 2 * body - front + group
            else:
                at = group - front
            table_ref[pl.ds(at * SUB, SUB), columns] = value
        for at in range(body + tail, 2 * body - front):
            table_ref[pl.ds(at * SUB, SUB), columns] = zero


def swap_blocks_and_bands(tiles):
    frames = SEG // HOP
    lane = lax.broadcasted_iota(jnp.int32, (SUB, SEG), 1)
    tiles = list(tiles)
    step = NB // 2
    while step:
        upper = ((lane // frames) & step) != 0
        for at in range(NB):
            if at & step:
                continue
            first, second = tiles[at], tiles[at + step]
            tiles[at] = jnp.where(upper, pltpu.roll(second, frames * step, axis=1), first)
            tiles[at + step] = jnp.where(upper, second, pltpu.roll(first, SEG - frames * step, axis=1))
        step //= 2
    return tiles


def amplitude_kernel(n_band, n_tile, xl_part, bins_ref, x_ref, out_ref, table_ref):
    fill_table(bins_ref, table_ref)
    table_high, table_low = split_halves(table_ref[...])
    blocks = NT // SEG
    group_bands = NB // n_band
    pitch = blocks * xl_part
    lane = lax.broadcasted_iota(jnp.int32, (SUB, SEG), 1)
    from_next = lane < WIN // 2 - HOP
    from_last = lane >= SEG - WIN // 2
    zero = jnp.zeros((SUB, SEG), jnp.float32)
    blank = jnp.zeros((RIM, NF), jnp.float32)
    for tile in range(n_tile):
        own, near = [], []
        for xl in range(xl_part):
            line = [
                x_ref[pl.ds(tile * SUB * pitch + block * xl_part + xl, SUB, stride=pitch), :]
                for block in range(blocks)
            ]
            for block in range(blocks):
                later = line[block + 1] if block + 1 < blocks else zero
                earlier = line[block - 1] if block else zero
                near.append(jnp.where(from_next, later, jnp.where(from_last, earlier, zero)))
            own += line
        high, low = split_halves(
            jnp.concatenate([jnp.concatenate(own, 0), jnp.concatenate(near, 0)], 1)
        )
        spectra = jnp.dot(high, table_high, preferred_element_type=jnp.float32)
        spectra += jnp.dot(low, table_high, preferred_element_type=jnp.float32)
        spectra += jnp.dot(high, table_low, preferred_element_type=jnp.float32)
        real_part, imag_part = spectra[:, :SEG], spectra[:, SEG:]
        amplitude = jnp.sqrt(real_part * real_part + imag_part * imag_part)
        for xl in range(xl_part):
            rows = [
                amplitude[(xl * blocks + block) * SUB : (xl * blocks + block + 1) * SUB]
                for block in range(blocks)
            ]
            for band, field in enumerate(swap_blocks_and_bands(rows)):
                group, inner = band // group_bands, band % group_bands

                def place(at):
                    return ((group * n_tile + at) * group_bands + inner) * xl_part + xl

                out_ref[place(tile), RIM : RIM + SUB] = field
                if tile + 1 < n_tile:
                    out_ref[place(tile + 1), :RIM] = field[SUB - RIM :]
                else:
                    out_ref[place(tile), RIM + SUB :] = blank
                if tile:
                    out_ref[place(tile - 1), RIM + SUB :] = field[:RIM]
                else:
                    out_ref[place(tile), :RIM] = blank


def fill_smoother(smoother_ref):
    row = lax.broadcasted_iota(jnp.int32, (NF, NF), 0)
    column = lax.broadcasted_iota(jnp.int32, (NF, NF), 1)
    band_matrix = jnp.zeros((NF, NF), jnp.float32)
    for k, weight in zip(range(-R, R + 1), stencil_weights()):
        band_matrix = jnp.where(row - column == k, weight, band_matrix)
    high, low = split_halves(band_matrix)
    smoother_ref[:NF, :NF] = high
    smoother_ref[:NF, NF:] = low
    smoother_ref[NF:, :NF] = high
    smoother_ref[NF:, NF:] = jnp.zeros((NF, NF), jnp.bfloat16)


def weighted(taps, scale):
    weights = [weight * scale for weight in stencil_weights()]
    total = weights[R] * taps[R]
    for k in range(1, R + 1):
        total += weights[R + k] * (taps[R - k] + taps[R + k])
    return total


def dips_kernel(group_bands, xl_part, xl_all, chunk, e_ref, out_ref, product_ref, row_ref, smoother_ref):
    fill_smoother(smoother_ref)
    lane = lax.broadcasted_iota(jnp.int32, (SUB, NF), 1)
    at_first, at_last = lane == 0, lane == NF - 1
    zero = jnp.zeros((SUB, NF), jnp.float32)
    low_rows, high_rows = 1, 2 * RIM - 1

    for band in range(group_bands):
        for k in range(R):
            for field in range(3):
                row_ref[field, band, k] = zero
                row_ref[field, band, xl_all + R + k] = zero

    def place(band, xl):
        return (xl // xl_part) * (group_bands * xl_part) + band * xl_part + xl % xl_part

    def products(step, carry):
        for band in range(group_bands):
            for inner in range(chunk):
                xl = step * chunk + inner
                here = place(band, xl)
                before = place(band, jnp.maximum(xl - 1, 0))
                after = place(band, jnp.minimum(xl + 1, xl_all - 1))
                slot = band * chunk + inner
                for half, start in enumerate((low_rows, high_rows)):
                    value = e_ref[here, start : start + SUB]
                    grad_il = e_ref[here, start + 1 : start + 1 + SUB] - e_ref[here, start - 1 : start - 1 + SUB]
                    right = e_ref[after, start : start + SUB]
                    left = e_ref[before, start : start + SUB]
                    if inner == 0:
                        left = jnp.where(xl > 0, left, zero)
                    if inner == chunk - 1:
                        right = jnp.where(xl < xl_all - 1, right, zero)
                    grad_xl = right - left
                    grad_time = jnp.where(at_last, zero, pltpu.roll(value, NF - 1, axis=1)) - jnp.where(
                        at_first, zero, pltpu.roll(value, 1, axis=1)
                    )
                    rows = slice(start - low_rows, start - low_rows + SUB)
                    product_ref[0, slot, rows] = grad_il * grad_time
                    product_ref[1, slot, rows] = grad_xl * grad_time
                    product_ref[2, slot, rows] = grad_time * grad_time
                for field in range(3):
                    taps = [product_ref[field, slot, k : k + SUB] for k in range(2 * R + 1)]
                    row_ref[field, band, xl + R] = weighted(taps, 0.25)
        return carry

    lax.fori_loop(0, xl_all // chunk, products, 0)

    def smooth(step, carry):
        for band in range(group_bands):
            fields = []
            for field in range(3):
                for inner in range(chunk):
                    xl = step * chunk + inner
                    fields.append(weighted([row_ref[field, band, xl + k] for k in range(2 * R + 1)], 1.0))
            high, low = split_halves(jnp.concatenate(fields, 0))
            both = jnp.concatenate([high, low], 1)
            tensor = jnp.dot(both, smoother_ref[...], preferred_element_type=jnp.float32)
            tensor = tensor[:, :NF] + tensor[:, NF:]
            size = chunk * SUB
            inverse = -1.0 / (tensor[2 * size :] + tiny_value)
            for field in range(2):
                dip = tensor[field * size : (field + 1) * size] * inverse
                for inner in range(chunk):
                    base = (band * 2 + field) * SUB * xl_all + step * chunk + inner
                    out_ref[pl.ds(base, SUB, stride=xl_all), :] = dip[inner * SUB : (inner + 1) * SUB]
        return carry

    lax.fori_loop(0, xl_all // chunk, smooth, 0)


def local(traces, bins):
    n_band = lax.axis_size("band")
    n_tile = lax.axis_size("tile")
    il_all, xl_part, _ = traces.shape
    tile_rows = il_all // n_tile
    group_bands = NB // n_band
    devices = n_band * n_tile
    xl_all = devices * xl_part
    blocks = NT // SEG
    window = tile_rows + 2 * RIM
    chunk = 8

    lines = traces.reshape(il_all, xl_part, blocks, SEG)
    lines = jnp.transpose(lines, (0, 2, 1, 3)).reshape(il_all * blocks * xl_part, SEG)
    vmem = pl.BlockSpec(memory_space=pltpu.VMEM)
    payload = pl.pallas_call(
        lambda *refs: amplitude_kernel(n_band, n_tile, xl_part, *refs),
        out_shape=jax.ShapeDtypeStruct((devices * group_bands * xl_part, window, NF), jnp.float32),
        in_specs=[pl.BlockSpec(memory_space=pltpu.SMEM), vmem],
        out_specs=vmem,
        scratch_shapes=[pltpu.VMEM((2 * SEG, 2 * SEG), jnp.float32)],
        compiler_params=pltpu.CompilerParams(vmem_limit_bytes=VMEM_LIMIT),
        name="amplitudes",
    )(bins, lines)
    payload = payload.reshape(devices, group_bands * xl_part, window, NF)
    bricks = lax.all_to_all(payload, ("band", "tile"), split_axis=0, concat_axis=0, tiled=True)
    dips = pl.pallas_call(
        lambda *refs: dips_kernel(group_bands, xl_part, xl_all, chunk, *refs),
        out_shape=jax.ShapeDtypeStruct((group_bands * 2 * tile_rows * xl_all, NF), jnp.float32),
        in_specs=[vmem],
        out_specs=vmem,
        scratch_shapes=[
            pltpu.VMEM((3, group_bands * chunk, 2 * RIM + SUB, NF), jnp.float32),
            pltpu.VMEM((3, group_bands, xl_all + 2 * R, SUB, NF), jnp.float32),
            pltpu.VMEM((2 * NF, 2 * NF), jnp.bfloat16),
        ],
        compiler_params=pltpu.CompilerParams(vmem_limit_bytes=VMEM_LIMIT),
        name="dips",
    )(bricks.reshape(devices * group_bands * xl_part, window, NF))
    return dips.reshape(group_bands, 2, tile_rows, xl_all, NF)


def solution(mesh):
    in_specs = (P(None, ("band", "tile"), None), P())
    out_specs = P("band", None, "tile", None, None)
    return jax.shard_map(local, mesh=mesh, in_specs=in_specs, out_specs=out_specs, check_vma=False)
```

time: 86.7 us -> 43.9 us (0.51)
  local copies, waits for them, and re-layouts: 30.5 us -> 1.7 us
  blocking collectives: 23.5 us -> 34.7 us
  other arithmetic: 10.2 us -> 0 us
  waiting for transfers between devices: 10.1 us -> 0 us
  Pallas kernels: 0 us -> 7.31 us
  matrix products: 7.15 us -> 0 us
  starting transfers between devices: 4.06 us -> 0 us
    gather x2 -> x0, local copies, waits for them, and re-layouts: 13.3 us -> none  [window_kernel(): picked = jnp.take(basis_rows, jnp.clip(offset, 0, WIN - 1), axis=2)]
    all_to_all x1, blocking collectives: 23.5 us -> 34.7 us  [local(): lax.all_to_all(payload, ('band', 'tile'), split_axis=0, concat_axis=0, ti...]
    ppermute x2 -> x0, waiting for transfers between devices: 10.1 us -> none  [the longest x1 10.1 us: extended_2(): lax.ppermute(lax.slice_in_dim(block, block.shape[dim] - width, None, axis...]
    another operation x11 -> x0, local copies, waits for them, and re-layouts: 9 us -> none  [the longest x9 5.66 us: band_amplitude(): jnp.stack([padded[:, :, block * SEG:block * SEG + seg_span] for block in...]
    pallas_call x0 -> x2, Pallas kernels: none -> 7.31 us  [the longest x1 5.76 us: local(): pl.pallas_call(lambda *refs: dips_kernel(group_bands, xl_part, xl_all, ch...]
    dot_general x1 -> x0, matrix products: 7.15 us -> none  [band_amplitude(): jnp.dot(pieces, dft_kernel, precision=lax.Precision.HIGHEST, preferred_el...]
    add x6 -> x0, other arithmetic: 4.46 us -> none  [smooth_axis(): result = scaled if result is None else result + scaled]
    ppermute x2 -> x0, starting transfers between devices: 4.06 us -> none  [the longest x1 2.77 us: extended_2(): lax.ppermute(lax.slice_in_dim(block, block.shape[dim] - width, None, axis...]
  transfers between devices with their start and end apart: 2 -> 0, of which waited for: 1 -> 0; matrix products, arithmetic and copies ran while one was open for 0% -> 0% of each run, Pallas kernels for 0% -> 0%
where the time goes in v1:
time: 43.9 us; the launch traced here: 43.7 us
  blocking collectives  34.7 us (79%)
  Pallas kernels  7.31 us (17%)
  local copies, waits for them, and re-layouts  1.7 us (4%)
    all_to_all x1, blocking collectives, local(): lax.all_to_all(payload, ('band', 'tile'), split_axis=0, concat_axis=0, ti...  34.7 us
    pallas_call x1, Pallas kernels, local(): pl.pallas_call(lambda *refs: dips_kernel(group_bands, xl_part, xl_all, ch...  5.76 us
    unnamed x4, local copies, waits for them, and re-layouts  1.7 us
    pallas_call x1, Pallas kernels, local(): pl.pallas_call(lambda *refs: amplitude_kernel(n_band, n_tile, xl_part, *r...  1.55 us

profile of v1, /device:TPU:0, one launch (start us, length us, event | category | flops | bytes accessed | tf_op | source)
XLA Modules:
  0.0 43.7 jit_solution(13737135045676965028)
XLA Ops:
  0.0 0.0 copy-start.1
  0.0 0.7 %copy-done.1 = s32[8]{0:T(128)S(1)} copy-done((s32[8]{0:T(128)S(1)}, s32[8]{0:T(128)}, u32[]{:S(2)}) %copy-start.1) | copy-done | bytes 56
  0.7 0.0 copy-start
  0.7 1.0 %copy-done = f32[64,2,1024]{2,1,0:T(2,128)S(1)} copy-done((f32[64,2,1024]{2,1,0:T(2,128)S(1)}, f32[64,2,1024]{2,1,0:T(2,128)}, u32[]{:S(2)}) %copy-start) | copy-done | bytes 524312
  1.7 1.6 %amplitudes.1 = f32[128,16,128]{2,1,0:T(8,128)S(1)} custom-call(s32[8]{0:T(128)S(1)} %copy-done.1, f32[1024,128]{1,0:T(8,128)S(1)} %bitcast.10), custom_call_target="tpu_custom_call" | custom-call | tf_op jit(solution)/shard_map/amplitudes/pallas_call | solution.py:265
  3.3 34.7 %all_to_all.5 = f32[32,4,16,128]{3,2,1,0:T(8,128)S(1)} all-to-all(f32[32,4,16,128]{3,2,1,0:T(8,128)S(1)} %bitcast.9), channel_id=1, replica_groups=mesh['band'=4,'tile'=8] {'band','tile'}, dimensions={0} | all-to-all | bytes 2097152 | tf_op jit(solution)/shard_map/all_to_all | solution.py:275
  38.0 5.8 %dips.1 = f32[2048,128]{1,0:T(8,128)} custom-call(f32[128,16,128]{2,1,0:T(8,128)S(1)} %bitcast.8), custom_call_target="tpu_custom_call" | custom-call | tf_op jit(solution)/shard_map/dips/pallas_call | solution.py:276
Async XLA Ops:
  0.0 0.7 %copy-start.1 = (s32[8]{0:T(128)S(1)}, s32[8]{0:T(128)}, u32[]{:S(2)}) copy-start(s32[8]{0:T(128)} %refs_0_.1) | copy-start | bytes 100
  0.7 1.0 %copy-start = (f32[64,2,1024]{2,1,0:T(2,128)S(1)}, f32[64,2,1024]{2,1,0:T(2,128)}, u32[]{:S(2)}) copy-start(f32[64,2,1024]{2,1,0:T(2,128)} %param.2) | copy-start | bytes 1572868

commit v2 on v1

--- a/solution.py
+++ b/solution.py
@@ -102,8 +102,16 @@
     return tiles
 
 
-def amplitude_kernel(n_band, n_tile, xl_part, bins_ref, x_ref, out_ref, table_ref):
+def amplitude_kernel(
+    n_band, n_tile, xl_part, far_bins_ref, far_ref, out_ref, table_ref, bins_ref, x_ref, bins_sem, x_sem
+):
+    bins_copy = pltpu.make_async_copy(far_bins_ref, bins_ref, bins_sem)
+    bins_copy.start()
+    x_copy = pltpu.make_async_copy(far_ref, x_ref, x_sem)
+    x_copy.start()
+    bins_copy.wait()
     fill_table(bins_ref, table_ref)
+    x_copy.wait()
     table_high, table_low = split_halves(table_ref[...])
     blocks = NT // SEG
     group_bands = NB // n_band
@@ -176,7 +184,9 @@
     return total
 
 
-def dips_kernel(group_bands, xl_part, xl_all, chunk, e_ref, out_ref, product_ref, row_ref, smoother_ref):
+def dips_kernel(
+    group_bands, xl_part, xl_all, chunk, e_ref, out_ref, stage_ref, product_ref, row_ref, smoother_ref, sent_ref
+):
     fill_smoother(smoother_ref)
     lane = lax.broadcasted_iota(jnp.int32, (SUB, NF), 1)
     at_first, at_last = lane == 0, lane == NF - 1
@@ -192,59 +202,71 @@
     def place(band, xl):
         return (xl // xl_part) * (group_bands * xl_part) + band * xl_part + xl % xl_part
 
-    def products(step, carry):
-        for band in range(group_bands):
+    def shifted_time(value):
+        later = jnp.where(at_last, zero, pltpu.roll(value, NF - 1, axis=1))
+        return later - jnp.where(at_first, zero, pltpu.roll(value, 1, axis=1))
+
+    def products(band, first):
+        lines = []
+        for xl in range(first - 1, first + chunk + 1):
+            if 0 <= xl < xl_all:
+                lines.append([e_ref[place(band, xl), s : s + SUB] for s in (low_rows, high_rows)])
+            else:
+                lines.append([zero, zero])
+        for inner in range(chunk):
+            xl = first + inner
+            here = place(band, xl)
+            slot = xl % (2 * chunk)
+            for half, start in enumerate((low_rows, high_rows)):
+                value = lines[inner + 1][half]
+                grad_il = e_ref[here, start + 1 : start + 1 + SUB] - e_ref[here, start - 1 : start - 1 + SUB]
+                grad_xl = lines[inner + 2][half] - lines[inner][half]
+                grad_time = shifted_time(value)
+                rows = slice(start - low_rows, start - low_rows + SUB)
+                product_ref[0, slot, rows] = grad_il * grad_time
+                product_ref[1, slot, rows] = grad_xl * grad_time
+                product_ref[2, slot, rows] = grad_time * grad_time
+            for field in range(3):
+                taps = [product_ref[field, slot, k : k + SUB] for k in range(2 * R + 1)]
+                row_ref[field, band, xl + R] = weighted(taps, 0.25)
+
+    def smooth(band, first):
+        slot = band * (xl_all // chunk) + first // chunk
+        fields = []
+        for field in range(3):
+            taps = [row_ref[field, band, first + k] for k in range(chunk + 2 * R)]
             for inner in range(chunk):
-                xl = step * chunk + inner
-                here = place(band, xl)
-                before = place(band, jnp.maximum(xl - 1, 0))
-                after = place(band, jnp.minimum(xl + 1, xl_all - 1))
-                slot = band * chunk + inner
-                for half, start in enumerate((low_rows, high_rows)):
-                    value = e_ref[here, start : start + SUB]
-                    grad_il = e_ref[here, start + 1 : start + 1 + SUB] - e_ref[here, start - 1 : start - 1 + SUB]
-                    right = e_ref[after, start : start + SUB]
-                    left = e_ref[before, start : start + SUB]
-                    if inner == 0:
-                        left = jnp.where(xl > 0, left, zero)
-                    if inner == chunk - 1:
-                        right = jnp.where(xl < xl_all - 1, right, zero)
-                    grad_xl = right - left
-                    grad_time = jnp.where(at_last, zero, pltpu.roll(value, NF - 1, axis=1)) - jnp.where(
-                        at_first, zero, pltpu.roll(value, 1, axis=1)
-                    )
-                    rows = slice(start - low_rows, start - low_rows + SUB)
-                    product_ref[0, slot, rows] = grad_il * grad_time
-                    product_ref[1, slot, rows] = grad_xl * grad_time
-                    product_ref[2, slot, rows] = grad_time * grad_time
-                for field in range(3):
-                    taps = [product_ref[field, slot, k : k + SUB] for k in range(2 * R + 1)]
-                    row_ref[field, band, xl + R] = weighted(taps, 0.25)
-        return carry
-
-    lax.fori_loop(0, xl_all // chunk, products, 0)
-
-    def smooth(step, carry):
-        for band in range(group_bands):
-            fields = []
-            for field in range(3):
-                for inner in range(chunk):
-                    xl = step * chunk + inner
-                    fields.append(weighted([row_ref[field, band, xl + k] for k in range(2 * R + 1)], 1.0))
-            high, low = split_halves(jnp.concatenate(fields, 0))
-            both = jnp.concatenate([high, low], 1)
-            tensor = jnp.dot(both, smoother_ref[...], preferred_element_type=jnp.float32)
-            tensor = tensor[:, :NF] + tensor[:, NF:]
-            size = chunk * SUB
-            inverse = -1.0 / (tensor[2 * size :] + tiny_value)
-            for field in range(2):
-                dip = tensor[field * size : (field + 1) * size] * inverse
-                for inner in range(chunk):
-                    base = (band * 2 + field) * SUB * xl_all + step * chunk + inner
-                    out_ref[pl.ds(base, SUB, stride=xl_all), :] = dip[inner * SUB : (inner + 1) * SUB]
-        return carry
-
-    lax.fori_loop(0, xl_all // chunk, smooth, 0)
+                fields.append(weighted(taps[inner : inner + 2 * R + 1], 1.0))
+        high, low = split_halves(jnp.concatenate(fields, 0))
+        both = jnp.concatenate([high, low], 1)
+        tensor = jnp.dot(both, smoother_ref[...], preferred_element_type=jnp.float32)
+        tensor = tensor[:, :NF] + tensor[:, NF:]
+        size = chunk * SUB
+        inverse = -1.0 / (tensor[2 * size :] + tiny_value)
+        for field in range(2):
+            dip = tensor[field * size : (field + 1) * size] * inverse
+            for inner in range(chunk):
+                rows = pl.ds(field * SUB * chunk + inner, SUB, stride=chunk)
+                stage_ref[slot, rows, :] = dip[inner * SUB : (inner + 1) * SUB]
+        copies = []
+        for at in range(2 * SUB):
+            copies.append(pltpu.make_async_copy(
+                stage_ref.at[slot, pl.ds(at * chunk, chunk)],
+                out_ref.at[pl.ds((band * 2 * SUB + at) * xl_all + first, chunk)],
+                sent_ref.at[slot],
+            ))
+            copies[-1].start()
+        return copies
+
+    copies = []
+    for band in range(group_bands):
+        for first in range(0, xl_all, chunk):
+            products(band, first)
+            if first:
+                copies += smooth(band, first - chunk)
+        copies += smooth(band, xl_all - chunk)
+    for copy in copies:
+        copy.wait()
 
 
 def local(traces, bins):
@@ -265,23 +287,32 @@
     payload = pl.pallas_call(
         lambda *refs: amplitude_kernel(n_band, n_tile, xl_part, *refs),
         out_shape=jax.ShapeDtypeStruct((devices * group_bands * xl_part, window, NF), jnp.float32),
-        in_specs=[pl.BlockSpec(memory_space=pltpu.SMEM), vmem],
+        in_specs=[pl.BlockSpec(memory_space=pltpu.HBM)] * 2,
         out_specs=vmem,
-        scratch_shapes=[pltpu.VMEM((2 * SEG, 2 * SEG), jnp.float32)],
+        scratch_shapes=[
+            pltpu.VMEM((2 * SEG, 2 * SEG), jnp.float32),
+            pltpu.SMEM(bins.shape, jnp.int32),
+            pltpu.VMEM(lines.shape, jnp.float32),
+            pltpu.SemaphoreType.DMA,
+            pltpu.SemaphoreType.DMA,
+        ],
         compiler_params=pltpu.CompilerParams(vmem_limit_bytes=VMEM_LIMIT),
         name="amplitudes",
-    )(bins, lines)
+    )(pltpu.with_memory_space_constraint(bins, pltpu.HBM), pltpu.with_memory_space_constraint(lines, pltpu.HBM))
     payload = payload.reshape(devices, group_bands * xl_part, window, NF)
     bricks = lax.all_to_all(payload, ("band", "tile"), split_axis=0, concat_axis=0, tiled=True)
+    steps = group_bands * xl_all // chunk
     dips = pl.pallas_call(
         lambda *refs: dips_kernel(group_bands, xl_part, xl_all, chunk, *refs),
         out_shape=jax.ShapeDtypeStruct((group_bands * 2 * tile_rows * xl_all, NF), jnp.float32),
         in_specs=[vmem],
-        out_specs=vmem,
+        out_specs=pl.BlockSpec(memory_space=pltpu.HBM),
         scratch_shapes=[
-            pltpu.VMEM((3, group_bands * chunk, 2 * RIM + SUB, NF), jnp.float32),
+            pltpu.VMEM((steps, 2 * SUB * chunk, NF), jnp.float32),
+            pltpu.VMEM((3, 2 * chunk, 2 * RIM + SUB, NF), jnp.float32),
             pltpu.VMEM((3, group_bands, xl_all + 2 * R, SUB, NF), jnp.float32),
             pltpu.VMEM((2 * NF, 2 * NF), jnp.bfloat16),
+            pltpu.SemaphoreType.DMA((steps,)),
         ],
         compiler_params=pltpu.CompilerParams(vmem_limit_bytes=VMEM_LIMIT),
         name="dips",

time: 43.9 us -> 39.6 us (0.902)
  Pallas kernels: 7.31 us -> 4.78 us
  local copies, waits for them, and re-layouts: 1.7 us -> 0 us
    pallas_call x1, Pallas kernels: 5.76 us -> 2.86 us  [local(): pl.pallas_call(lambda *refs: dips_kernel(group_bands, xl_part, xl_all, ch...]
    unnamed x4 -> x0, local copies, waits for them, and re-layouts: 1.7 us -> none
where the time goes in v2:
time: 39.6 us; the launch traced here: 39.5 us
  blocking collectives  34.7 us (88%)
  Pallas kernels  4.78 us (12%)
    all_to_all x1, blocking collectives, local(): lax.all_to_all(payload, ('band', 'tile'), split_axis=0, concat_axis=0, ti...  34.7 us
    pallas_call x1, Pallas kernels, local(): pl.pallas_call(lambda *refs: dips_kernel(group_bands, xl_part, xl_all, ch...  2.86 us
    pallas_call x1, Pallas kernels, local(): pl.pallas_call(lambda *refs: amplitude_kernel(n_band, n_tile, xl_part, *r...  1.92 us

profile of v2, /device:TPU:0, one launch (start us, length us, event | category | flops | bytes accessed | tf_op | source)
XLA Modules:
  0.0 39.5 jit_solution(16605076789099234067)
XLA Ops:
  0.0 1.9 %amplitudes.1 = f32[128,16,128]{2,1,0:T(8,128)S(1)} custom-call(s32[8]{0:T(128)} %refs_0_.1, f32[1024,128]{1,0:T(8,128)} %bitcast.10), custom_call_target="tpu_custom_call" | custom-call | tf_op jit(solution)/shard_map/amplitudes/pallas_call | solution.py:287
  1.9 34.7 %all_to_all.5 = f32[32,4,16,128]{3,2,1,0:T(8,128)S(1)} all-to-all(f32[32,4,16,128]{3,2,1,0:T(8,128)S(1)} %bitcast.9), channel_id=1, replica_groups=mesh['band'=4,'tile'=8] {'band','tile'}, dimensions={0} | all-to-all | bytes 2097152 | tf_op jit(solution)/shard_map/all_to_all | solution.py:303
  36.6 2.9 %dips.1 = f32[2048,128]{1,0:T(8,128)} custom-call(f32[128,16,128]{2,1,0:T(8,128)S(1)} %bitcast.8), custom_call_target="tpu_custom_call" | custom-call | tf_op jit(solution)/shard_map/dips/pallas_call | solution.py:305

commit v3 on v2

--- a/solution.py
+++ b/solution.py
@@ -102,6 +102,14 @@
     return tiles
 
 
+def exchange_order(n_band, n_tile):
+    order = []
+    for step in range(2 * n_band):
+        last, band = divmod(step ^ (step >> 1), n_band)
+        order += [band * n_tile + tile for tile in range(last, n_tile, 2)]
+    return order
+
+
 def amplitude_kernel(
     n_band, n_tile, xl_part, far_bins_ref, far_ref, out_ref, table_ref, bins_ref, x_ref, bins_sem, x_sem
 ):
@@ -115,6 +123,7 @@
     table_high, table_low = split_halves(table_ref[...])
     blocks = NT // SEG
     group_bands = NB // n_band
+    order = exchange_order(n_band, n_tile)
     pitch = blocks * xl_part
     lane = lax.broadcasted_iota(jnp.int32, (SUB, SEG), 1)
     from_next = lane < WIN // 2 - HOP
@@ -150,7 +159,7 @@
                 group, inner = band // group_bands, band % group_bands
 
                 def place(at):
-                    return ((group * n_tile + at) * group_bands + inner) * xl_part + xl
+                    return (order.index(group * n_tile + at) * group_bands + inner) * xl_part + xl
 
                 out_ref[place(tile), RIM : RIM + SUB] = field
                 if tile + 1 < n_tile:
@@ -185,7 +194,7 @@
 
 
 def dips_kernel(
-    group_bands, xl_part, xl_all, chunk, e_ref, out_ref, stage_ref, product_ref, row_ref, smoother_ref, sent_ref
+    order, group_bands, xl_part, xl_all, chunk, e_ref, out_ref, stage_ref, product_ref, row_ref, smoother_ref, sent_ref
 ):
     fill_smoother(smoother_ref)
     lane = lax.broadcasted_iota(jnp.int32, (SUB, NF), 1)
@@ -200,7 +209,7 @@
                 row_ref[field, band, xl_all + R + k] = zero
 
     def place(band, xl):
-        return (xl // xl_part) * (group_bands * xl_part) + band * xl_part + xl % xl_part
+        return order.index(xl // xl_part) * (group_bands * xl_part) + band * xl_part + xl % xl_part
 
     def shifted_time(value):
         later = jnp.where(at_last, zero, pltpu.roll(value, NF - 1, axis=1))
@@ -276,6 +285,7 @@
     tile_rows = il_all // n_tile
     group_bands = NB // n_band
     devices = n_band * n_tile
+    order = exchange_order(n_band, n_tile)
     xl_all = devices * xl_part
     blocks = NT // SEG
     window = tile_rows + 2 * RIM
@@ -300,10 +310,12 @@
         name="amplitudes",
     )(pltpu.with_memory_space_constraint(bins, pltpu.HBM), pltpu.with_memory_space_constraint(lines, pltpu.HBM))
     payload = payload.reshape(devices, group_bands * xl_part, window, NF)
-    bricks = lax.all_to_all(payload, ("band", "tile"), split_axis=0, concat_axis=0, tiled=True)
+    bricks = lax.all_to_all(
+        payload, ("band", "tile"), split_axis=0, concat_axis=0, axis_index_groups=[order], tiled=True
+    )
     steps = group_bands * xl_all // chunk
     dips = pl.pallas_call(
-        lambda *refs: dips_kernel(group_bands, xl_part, xl_all, chunk, *refs),
+        lambda *refs: dips_kernel(order, group_bands, xl_part, xl_all, chunk, *refs),
         out_shape=jax.ShapeDtypeStruct((group_bands * 2 * tile_rows * xl_all, NF), jnp.float32),
         in_specs=[vmem],
         out_specs=pl.BlockSpec(memory_space=pltpu.HBM),

time: 39.6 us -> 37.9 us (0.957)
  blocking collectives: 34.7 us -> 32.6 us
    all_to_all x1, blocking collectives: 34.7 us -> 32.6 us  [local(): lax.all_to_all(payload, ('band', 'tile'), split_axis=0, concat_axis=0, ax...]
where the time goes in v3:
time: 37.9 us; the launch traced here: 37.4 us
  blocking collectives  32.6 us (86%)
  Pallas kernels  4.78 us (13%)
    all_to_all x1, blocking collectives, local(): lax.all_to_all(payload, ('band', 'tile'), split_axis=0, concat_axis=0, ax...  32.6 us
    pallas_call x1, Pallas kernels, local(): pl.pallas_call(lambda *refs: dips_kernel(order, group_bands, xl_part, xl_...  2.86 us
    pallas_call x1, Pallas kernels, local(): pl.pallas_call(lambda *refs: amplitude_kernel(n_band, n_tile, xl_part, *r...  1.92 us

profile of v3, /device:TPU:0, one launch (start us, length us, event | category | flops | bytes accessed | tf_op | source)
XLA Modules:
  0.0 37.4 jit_solution(5243275860894159916)
XLA Ops:
  0.0 1.9 %amplitudes.1 = f32[128,16,128]{2,1,0:T(8,128)S(1)} custom-call(s32[8]{0:T(128)} %refs_0_.1, f32[1024,128]{1,0:T(8,128)} %bitcast.10), custom_call_target="tpu_custom_call" | custom-call | tf_op jit(solution)/shard_map/amplitudes/pallas_call | solution.py:297
  1.9 32.6 %all_to_all.5 = f32[32,4,16,128]{3,2,1,0:T(8,128)S(1)} all-to-all(f32[32,4,16,128]{3,2,1,0:T(8,128)S(1)} %bitcast.9), channel_id=1, replica_groups={{0,2,4,6,8,10,12,14,24,26,28,30,16,18,20,22,17,19,21,23,25,27,29,31,9,1..., dimensions={0} | all-to-all | bytes 2097152 | tf_op jit(solution)/shard_map/all_to_all | solution.py:313
  34.5 2.9 %dips.1 = f32[2048,128]{1,0:T(8,128)} custom-call(f32[128,16,128]{2,1,0:T(8,128)S(1)} %bitcast.8), custom_call_target="tpu_custom_call" | custom-call | tf_op jit(solution)/shard_map/dips/pallas_call | solution.py:317

commit v4 on v3

--- a/solution.py
+++ b/solution.py
@@ -103,10 +103,12 @@
 
 
 def exchange_order(n_band, n_tile):
+    count = n_tile // 2
+    line = [1, 0, *range(2, count)]
     order = []
     for step in range(2 * n_band):
         last, band = divmod(step ^ (step >> 1), n_band)
-        order += [band * n_tile + tile for tile in range(last, n_tile, 2)]
+        order += [band * n_tile + 2 * line[(at - step) % count] + last for at in range(count)]
     return order
 
 
@@ -176,8 +178,10 @@
     row = lax.broadcasted_iota(jnp.int32, (NF, NF), 0)
     column = lax.broadcasted_iota(jnp.int32, (NF, NF), 1)
     band_matrix = jnp.zeros((NF, NF), jnp.float32)
-    for k, weight in zip(range(-R, R + 1), stencil_weights()):
-        band_matrix = jnp.where(row - column == k, weight, band_matrix)
+    weights = stencil_weights()
+    scale = 0.25 * weights[R] * weights[R]
+    for k, weight in zip(range(-R, R + 1), weights):
+        band_matrix = jnp.where(row - column == k, weight * scale, band_matrix)
     high, low = split_halves(band_matrix)
     smoother_ref[:NF, :NF] = high
     smoother_ref[:NF, NF:] = low
@@ -185,11 +189,11 @@
     smoother_ref[NF:, NF:] = jnp.zeros((NF, NF), jnp.bfloat16)
 
 
-def weighted(taps, scale):
-    weights = [weight * scale for weight in stencil_weights()]
-    total = weights[R] * taps[R]
+def weighted(taps):
+    weights = stencil_weights()
+    total = taps[R]
     for k in range(1, R + 1):
-        total += weights[R + k] * (taps[R - k] + taps[R + k])
+        total += (weights[R + k] / weights[R]) * (taps[R - k] + taps[R + k])
     return total
 
 
@@ -237,7 +241,7 @@
                 product_ref[2, slot, rows] = grad_time * grad_time
             for field in range(3):
                 taps = [product_ref[field, slot, k : k + SUB] for k in range(2 * R + 1)]
-                row_ref[field, band, xl + R] = weighted(taps, 0.25)
+                row_ref[field, band, xl + R] = weighted(taps)
 
     def smooth(band, first):
         slot = band * (xl_all // chunk) + first // chunk
@@ -245,7 +249,7 @@
         for field in range(3):
             taps = [row_ref[field, band, first + k] for k in range(chunk + 2 * R)]
             for inner in range(chunk):
-                fields.append(weighted(taps[inner : inner + 2 * R + 1], 1.0))
+                fields.append(weighted(taps[inner : inner + 2 * R + 1]))
         high, low = split_halves(jnp.concatenate(fields, 0))
         both = jnp.concatenate([high, low], 1)
         tensor = jnp.dot(both, smoother_ref[...], preferred_element_type=jnp.float32)
@@ -257,23 +261,21 @@
             for inner in range(chunk):
                 rows = pl.ds(field * SUB * chunk + inner, SUB, stride=chunk)
                 stage_ref[slot, rows, :] = dip[inner * SUB : (inner + 1) * SUB]
-        copies = []
-        for at in range(2 * SUB):
-            copies.append(pltpu.make_async_copy(
-                stage_ref.at[slot, pl.ds(at * chunk, chunk)],
-                out_ref.at[pl.ds((band * 2 * SUB + at) * xl_all + first, chunk)],
-                sent_ref.at[slot],
-            ))
-            copies[-1].start()
-        return copies
+        copy = pltpu.make_async_copy(
+            stage_ref.at[slot].reshape(2 * SUB, chunk, NF),
+            out_ref.at[pl.ds(band * 2 * SUB, 2 * SUB), pl.ds(first, chunk)],
+            sent_ref.at[slot],
+        )
+        copy.start()
+        return copy
 
     copies = []
     for band in range(group_bands):
         for first in range(0, xl_all, chunk):
             products(band, first)
             if first:
-                copies += smooth(band, first - chunk)
-        copies += smooth(band, xl_all - chunk)
+                copies.append(smooth(band, first - chunk))
+        copies.append(smooth(band, xl_all - chunk))
     for copy in copies:
         copy.wait()
 
@@ -316,7 +318,7 @@
     steps = group_bands * xl_all // chunk
     dips = pl.pallas_call(
         lambda *refs: dips_kernel(order, group_bands, xl_part, xl_all, chunk, *refs),
-        out_shape=jax.ShapeDtypeStruct((group_bands * 2 * tile_rows * xl_all, NF), jnp.float32),
+        out_shape=jax.ShapeDtypeStruct((group_bands * 2 * tile_rows, xl_all, NF), jnp.float32),
         in_specs=[vmem],
         out_specs=pl.BlockSpec(memory_space=pltpu.HBM),
         scratch_shapes=[

time: 37.9 us -> 36.7 us (0.968)
  blocking collectives: 32.6 us -> 31.4 us
    all_to_all x1, blocking collectives: 32.6 us -> 31.4 us  [local(): lax.all_to_all(payload, ('band', 'tile'), split_axis=0, concat_axis=0, ax...]
where the time goes in v4:
time: 36.7 us; the launch traced here: 36.1 us
  blocking collectives  31.4 us (86%)
  Pallas kernels  4.67 us (13%)
    all_to_all x1, blocking collectives, local(): lax.all_to_all(payload, ('band', 'tile'), split_axis=0, concat_axis=0, ax...  31.4 us
    pallas_call x1, Pallas kernels, local(): pl.pallas_call(lambda *refs: dips_kernel(order, group_bands, xl_part, xl_...  2.75 us
    pallas_call x1, Pallas kernels, local(): pl.pallas_call(lambda *refs: amplitude_kernel(n_band, n_tile, xl_part, *r...  1.92 us

profile of v4, /device:TPU:0, one launch (start us, length us, event | category | flops | bytes accessed | tf_op | source)
XLA Modules:
  0.0 36.1 jit_solution(846213530556042579)
XLA Ops:
  0.0 1.9 %amplitudes.1 = f32[128,16,128]{2,1,0:T(8,128)S(1)} custom-call(s32[8]{0:T(128)} %refs_0_.1, f32[1024,128]{1,0:T(8,128)} %bitcast.10), custom_call_target="tpu_custom_call" | custom-call | tf_op jit(solution)/shard_map/amplitudes/pallas_call | solution.py:299
  1.9 31.4 %all_to_all.5 = f32[32,4,16,128]{3,2,1,0:T(8,128)S(1)} all-to-all(f32[32,4,16,128]{3,2,1,0:T(8,128)S(1)} %bitcast.9), channel_id=1, replica_groups={{2,0,4,6,14,10,8,12,28,30,26,24,16,20,22,18,19,17,21,23,31,27,25,29,13,..., dimensions={0} | all-to-all | bytes 2097152 | tf_op jit(solution)/shard_map/all_to_all | solution.py:315
  33.4 2.7 %dips.1 = f32[32,64,128]{2,1,0:T(8,128)} custom-call(f32[128,16,128]{2,1,0:T(8,128)S(1)} %bitcast.8), custom_call_target="tpu_custom_call" | custom-call | tf_op jit(solution)/shard_map/dips/pallas_call | solution.py:319

commit v5 on v4

--- a/solution.py
+++ b/solution.py
@@ -87,19 +87,15 @@
 
 def swap_blocks_and_bands(tiles):
     frames = SEG // HOP
-    lane = lax.broadcasted_iota(jnp.int32, (SUB, SEG), 1)
-    tiles = list(tiles)
-    step = NB // 2
-    while step:
-        upper = ((lane // frames) & step) != 0
-        for at in range(NB):
-            if at & step:
-                continue
-            first, second = tiles[at], tiles[at + step]
-            tiles[at] = jnp.where(upper, pltpu.roll(second, frames * step, axis=1), first)
-            tiles[at + step] = jnp.where(upper, second, pltpu.roll(first, SEG - frames * step, axis=1))
-        step //= 2
-    return tiles
+    group = lax.broadcasted_iota(jnp.int32, (SUB, SEG), 1) // frames
+    tiles = [tiles[0]] + [pltpu.roll(tiles[at], frames * at, axis=1) for at in range(1, NB)]
+    step = 1
+    while step < NB:
+        moved = (group & step) != 0
+        tiles = [jnp.where(moved, tiles[(at + step) % NB], tiles[at]) for at in range(NB)]
+        step *= 2
+    tiles = [tiles[-band % NB] for band in range(NB)]
+    return [tiles[0]] + [pltpu.roll(tiles[band], SEG - frames * band, axis=1) for band in range(1, NB)]
 
 
 def exchange_order(n_band, n_tile):
@@ -229,7 +225,7 @@
         for inner in range(chunk):
             xl = first + inner
             here = place(band, xl)
-            slot = xl % (2 * chunk)
+            slot = band * xl_all + xl
             for half, start in enumerate((low_rows, high_rows)):
                 value = lines[inner + 1][half]
                 grad_il = e_ref[here, start + 1 : start + 1 + SUB] - e_ref[here, start - 1 : start - 1 + SUB]
@@ -323,7 +319,7 @@
         out_specs=pl.BlockSpec(memory_space=pltpu.HBM),
         scratch_shapes=[
             pltpu.VMEM((steps, 2 * SUB * chunk, NF), jnp.float32),
-            pltpu.VMEM((3, 2 * chunk, 2 * RIM + SUB, NF), jnp.float32),
+            pltpu.VMEM((3, group_bands * xl_all, 2 * RIM + SUB, NF), jnp.float32),
             pltpu.VMEM((3, group_bands, xl_all + 2 * R, SUB, NF), jnp.float32),
             pltpu.VMEM((2 * NF, 2 * NF), jnp.bfloat16),
             pltpu.SemaphoreType.DMA((steps,)),

time: 36.7 us -> 36.6 us (level)
  no operation moved by 1% of the time
where the time goes in v5:
time: 36.6 us; the launch traced here: 36 us
  blocking collectives  31.4 us (86%)
  Pallas kernels  4.61 us (13%)
    all_to_all x1, blocking collectives, local(): lax.all_to_all(payload, ('band', 'tile'), split_axis=0, concat_axis=0, ax...  31.4 us
    pallas_call x1, Pallas kernels, local(): pl.pallas_call(lambda *refs: dips_kernel(order, group_bands, xl_part, xl_...  2.73 us
    pallas_call x1, Pallas kernels, local(): pl.pallas_call(lambda *refs: amplitude_kernel(n_band, n_tile, xl_part, *r...  1.88 us

profile of v5, /device:TPU:0, one launch (start us, length us, event | category | flops | bytes accessed | tf_op | source)
XLA Modules:
  0.0 36.0 jit_solution(408399011441270343)
XLA Ops:
  0.0 1.9 %amplitudes.1 = f32[128,16,128]{2,1,0:T(8,128)S(1)} custom-call(s32[8]{0:T(128)} %refs_0_.1, f32[1024,128]{1,0:T(8,128)} %bitcast.10), custom_call_target="tpu_custom_call" | custom-call | tf_op jit(solution)/shard_map/amplitudes/pallas_call | solution.py:295
  1.9 31.4 %all_to_all.5 = f32[32,4,16,128]{3,2,1,0:T(8,128)S(1)} all-to-all(f32[32,4,16,128]{3,2,1,0:T(8,128)S(1)} %bitcast.9), channel_id=1, replica_groups={{2,0,4,6,14,10,8,12,28,30,26,24,16,20,22,18,19,17,21,23,31,27,25,29,13,..., dimensions={0} | all-to-all | bytes 2097152 | tf_op jit(solution)/shard_map/all_to_all | solution.py:311
  33.3 2.7 %dips.1 = f32[32,64,128]{2,1,0:T(8,128)} custom-call(f32[128,16,128]{2,1,0:T(8,128)S(1)} %bitcast.8), custom_call_target="tpu_custom_call" | custom-call | tf_op jit(solution)/shard_map/dips/pallas_call | solution.py:315

commit v6 on v5

--- a/solution.py
+++ b/solution.py
@@ -48,6 +48,14 @@
     high = value.astype(jnp.bfloat16)
     low = (value - high.astype(jnp.float32)).astype(jnp.bfloat16)
     return high, low
+
+
+def split_parts(value, count):
+    parts = []
+    for _ in range(count):
+        parts.append(value.astype(jnp.bfloat16))
+        value = value - parts[-1].astype(jnp.float32)
+    return parts
 
 
 def fill_table(bins_ref, table_ref):
@@ -118,7 +126,7 @@
     bins_copy.wait()
     fill_table(bins_ref, table_ref)
     x_copy.wait()
-    table_high, table_low = split_halves(table_ref[...])
+    table = split_parts(table_ref[...], 3)
     blocks = NT // SEG
     group_bands = NB // n_band
     order = exchange_order(n_band, n_tile)
@@ -140,12 +148,15 @@
                 earlier = line[block - 1] if block else zero
                 near.append(jnp.where(from_next, later, jnp.where(from_last, earlier, zero)))
             own += line
-        high, low = split_halves(
-            jnp.concatenate([jnp.concatenate(own, 0), jnp.concatenate(near, 0)], 1)
-        )
-        spectra = jnp.dot(high, table_high, preferred_element_type=jnp.float32)
-        spectra += jnp.dot(low, table_high, preferred_element_type=jnp.float32)
-        spectra += jnp.dot(high, table_low, preferred_element_type=jnp.float32)
+        samples = split_parts(jnp.concatenate([jnp.concatenate(own, 0), jnp.concatenate(near, 0)], 1), 3)
+        spectra = None
+        for at in (2, 1, 0):
+            count = 3 - at
+            term = jnp.dot(jnp.concatenate(samples[:count], 0), table[at], preferred_element_type=jnp.float32)
+            size = term.shape[0] // count
+            for piece in reversed(range(count)):
+                part = term[piece * size : (piece + 1) * size]
+                spectra = part if spectra is None else spectra + part
         real_part, imag_part = spectra[:, :SEG], spectra[:, SEG:]
         amplitude = jnp.sqrt(real_part * real_part + imag_part * imag_part)
         for xl in range(xl_part):

time: 36.6 us -> 37 us (1.011)
  Pallas kernels: 4.61 us -> 4.99 us
    pallas_call x1, Pallas kernels: 1.88 us -> 2.25 us  [local(): pl.pallas_call(lambda *refs: amplitude_kernel(n_band, n_tile, xl_part, *r...]
where the time goes in v6:
time: 37 us; the launch traced here: 36.4 us
  blocking collectives  31.4 us (85%)
  Pallas kernels  4.99 us (13%)
    all_to_all x1, blocking collectives, local(): lax.all_to_all(payload, ('band', 'tile'), split_axis=0, concat_axis=0, ax...  31.4 us
    pallas_call x1, Pallas kernels, local(): pl.pallas_call(lambda *refs: dips_kernel(order, group_bands, xl_part, xl_...  2.73 us
    pallas_call x1, Pallas kernels, local(): pl.pallas_call(lambda *refs: amplitude_kernel(n_band, n_tile, xl_part, *r...  2.25 us

profile of v6, /device:TPU:0, one launch (start us, length us, event | category | flops | bytes accessed | tf_op | source)
XLA Modules:
  0.0 36.4 jit_solution(5965583133027384910)
XLA Ops:
  0.0 2.3 %amplitudes.1 = f32[128,16,128]{2,1,0:T(8,128)S(1)} custom-call(s32[8]{0:T(128)} %refs_0_.1, f32[1024,128]{1,0:T(8,128)} %bitcast.10), custom_call_target="tpu_custom_call" | custom-call | tf_op jit(solution)/shard_map/amplitudes/pallas_call | solution.py:306
  2.3 31.4 %all_to_all.5 = f32[32,4,16,128]{3,2,1,0:T(8,128)S(1)} all-to-all(f32[32,4,16,128]{3,2,1,0:T(8,128)S(1)} %bitcast.9), channel_id=1, replica_groups={{2,0,4,6,14,10,8,12,28,30,26,24,16,20,22,18,19,17,21,23,31,27,25,29,13,..., dimensions={0} | all-to-all | bytes 2097152 | tf_op jit(solution)/shard_map/all_to_all | solution.py:322
  33.7 2.7 %dips.1 = f32[32,64,128]{2,1,0:T(8,128)} custom-call(f32[128,16,128]{2,1,0:T(8,128)S(1)} %bitcast.8), custom_call_target="tpu_custom_call" | custom-call | tf_op jit(solution)/shard_map/dips/pallas_call | solution.py:326

commit v7 on v6

--- a/solution.py
+++ b/solution.py
@@ -108,11 +108,12 @@
 
 def exchange_order(n_band, n_tile):
     count = n_tile // 2
-    line = [1, 0, *range(2, count)]
+    line = [1, 2, 0, *range(3, count)]
+    turns = (0, 3, 0, 3, 0, 3, 2, 1)
     order = []
     for step in range(2 * n_band):
         last, band = divmod(step ^ (step >> 1), n_band)
-        order += [band * n_tile + 2 * line[(at - step) % count] + last for at in range(count)]
+        order += [band * n_tile + 2 * line[(at + turns[step % len(turns)]) % count] + last for at in range(count)]
     return order
 
 
@@ -125,8 +126,8 @@
     x_copy.start()
     bins_copy.wait()
     fill_table(bins_ref, table_ref)
+    table = split_parts(table_ref[...], 3)
     x_copy.wait()
-    table = split_parts(table_ref[...], 3)
     blocks = NT // SEG
     group_bands = NB // n_band
     order = exchange_order(n_band, n_tile)

time: 37 us -> 36.7 us (level)
  the two profiles are of different devices: /device:TPU:0 before, /device:TPU:3 now
where the time goes in v7:
time: 36.7 us; the launch traced here: 36.5 us
  blocking collectives  31.6 us (86%)
  Pallas kernels  4.96 us (14%)
    all_to_all x1, blocking collectives, local(): lax.all_to_all(payload, ('band', 'tile'), split_axis=0, concat_axis=0, ax...  31.6 us
    pallas_call x1, Pallas kernels, local(): pl.pallas_call(lambda *refs: dips_kernel(order, group_bands, xl_part, xl_...  2.73 us
    pallas_call x1, Pallas kernels, local(): pl.pallas_call(lambda *refs: amplitude_kernel(n_band, n_tile, xl_part, *r...  2.23 us

profile of v7, /device:TPU:3, one launch (start us, length us, event | category | flops | bytes accessed | tf_op | source)
XLA Modules:
  0.0 36.5 jit_solution(17821187726833246950)
XLA Ops:
  0.0 2.2 %amplitudes.1 = f32[128,16,128]{2,1,0:T(8,128)S(1)} custom-call(s32[8]{0:T(128)} %refs_0_.1, f32[1024,128]{1,0:T(8,128)} %bitcast.10), custom_call_target="tpu_custom_call" | custom-call | tf_op jit(solution)/shard_map/amplitudes/pallas_call | solution.py:307
  2.2 31.6 %all_to_all.5 = f32[32,4,16,128]{3,2,1,0:T(8,128)S(1)} all-to-all(f32[32,4,16,128]{3,2,1,0:T(8,128)S(1)} %bitcast.9), channel_id=1, replica_groups={{2,4,0,6,14,10,12,8,26,28,24,30,22,18,20,16,19,21,17,23,31,27,29,25,9,1..., dimensions={0} | all-to-all | bytes 2097152 | tf_op jit(solution)/shard_map/all_to_all | solution.py:323
  33.8 2.7 %dips.1 = f32[32,64,128]{2,1,0:T(8,128)} custom-call(f32[128,16,128]{2,1,0:T(8,128)S(1)} %bitcast.8), custom_call_target="tpu_custom_call" | custom-call | tf_op jit(solution)/shard_map/dips/pallas_call | solution.py:327

commit v8 on v7

--- a/solution.py
+++ b/solution.py
@@ -137,18 +137,19 @@
     from_last = lane >= SEG - WIN // 2
     zero = jnp.zeros((SUB, SEG), jnp.float32)
     blank = jnp.zeros((RIM, NF), jnp.float32)
-    for tile in range(n_tile):
+    for first in range(0, n_tile, n_tile):
         own, near = [], []
-        for xl in range(xl_part):
-            line = [
-                x_ref[pl.ds(tile * SUB * pitch + block * xl_part + xl, SUB, stride=pitch), :]
-                for block in range(blocks)
-            ]
-            for block in range(blocks):
-                later = line[block + 1] if block + 1 < blocks else zero
-                earlier = line[block - 1] if block else zero
-                near.append(jnp.where(from_next, later, jnp.where(from_last, earlier, zero)))
-            own += line
+        for tile in range(first, first + n_tile):
+            for xl in range(xl_part):
+                line = [
+                    x_ref[pl.ds(tile * SUB * pitch + block * xl_part + xl, SUB, stride=pitch), :]
+                    for block in range(blocks)
+                ]
+                for block in range(blocks):
+                    later = line[block + 1] if block + 1 < blocks else zero
+                    earlier = line[block - 1] if block else zero
+                    near.append(jnp.where(from_next, later, jnp.where(from_last, earlier, zero)))
+                own += line
         samples = split_parts(jnp.concatenate([jnp.concatenate(own, 0), jnp.concatenate(near, 0)], 1), 3)
         spectra = None
         for at in (2, 1, 0):
@@ -160,26 +161,25 @@
                 spectra = part if spectra is None else spectra + part
         real_part, imag_part = spectra[:, :SEG], spectra[:, SEG:]
         amplitude = jnp.sqrt(real_part * real_part + imag_part * imag_part)
-        for xl in range(xl_part):
-            rows = [
-                amplitude[(xl * blocks + block) * SUB : (xl * blocks + block + 1) * SUB]
-                for block in range(blocks)
-            ]
-            for band, field in enumerate(swap_blocks_and_bands(rows)):
-                group, inner = band // group_bands, band % group_bands
-
-                def place(at):
-                    return (order.index(group * n_tile + at) * group_bands + inner) * xl_part + xl
-
-                out_ref[place(tile), RIM : RIM + SUB] = field
-                if tile + 1 < n_tile:
-                    out_ref[place(tile + 1), :RIM] = field[SUB - RIM :]
-                else:
-                    out_ref[place(tile), RIM + SUB :] = blank
-                if tile:
-                    out_ref[place(tile - 1), RIM + SUB :] = field[:RIM]
-                else:
-                    out_ref[place(tile), :RIM] = blank
+        for tile in range(first, first + n_tile):
+            for xl in range(xl_part):
+                at = ((tile - first) * xl_part + xl) * blocks
+                rows = [amplitude[(at + block) * SUB : (at + block + 1) * SUB] for block in range(blocks)]
+                for band, field in enumerate(swap_blocks_and_bands(rows)):
+                    group, inner = band // group_bands, band % group_bands
+
+                    def place(at):
+                        return (order.index(group * n_tile + at) * group_bands + inner) * xl_part + xl
+
+                    out_ref[place(tile), RIM : RIM + SUB] = field
+                    if tile + 1 < n_tile:
+                        out_ref[place(tile + 1), :RIM] = field[SUB - RIM :]
+                    else:
+                        out_ref[place(tile), RIM + SUB :] = blank
+                    if tile:
+                        out_ref[place(tile - 1), RIM + SUB :] = field[:RIM]
+                    else:
+                        out_ref[place(tile), :RIM] = blank
 
 
 def fill_smoother(smoother_ref):

time: 36.7 us -> 36.7 us (level)
  no operation moved by 1% of the time
where the time goes in v8:
time: 36.7 us; the launch traced here: 36.5 us
  blocking collectives  31.6 us (86%)
  Pallas kernels  4.95 us (13%)
    all_to_all x1, blocking collectives, local(): lax.all_to_all(payload, ('band', 'tile'), split_axis=0, concat_axis=0, ax...  31.6 us
    pallas_call x1, Pallas kernels, local(): pl.pallas_call(lambda *refs: dips_kernel(order, group_bands, xl_part, xl_...  2.73 us
    pallas_call x1, Pallas kernels, local(): pl.pallas_call(lambda *refs: amplitude_kernel(n_band, n_tile, xl_part, *r...  2.22 us

profile of v8, /device:TPU:3, one launch (start us, length us, event | category | flops | bytes accessed | tf_op | source)
XLA Modules:
  0.0 36.5 jit_solution(5639035655902901884)
XLA Ops:
  0.0 2.2 %amplitudes.1 = f32[128,16,128]{2,1,0:T(8,128)S(1)} custom-call(s32[8]{0:T(128)} %refs_0_.1, f32[1024,128]{1,0:T(8,128)} %bitcast.10), custom_call_target="tpu_custom_call" | custom-call | tf_op jit(solution)/shard_map/amplitudes/pallas_call | solution.py:307
  2.2 31.6 %all_to_all.5 = f32[32,4,16,128]{3,2,1,0:T(8,128)S(1)} all-to-all(f32[32,4,16,128]{3,2,1,0:T(8,128)S(1)} %bitcast.9), channel_id=1, replica_groups={{2,4,0,6,14,10,12,8,26,28,24,30,22,18,20,16,19,21,17,23,31,27,29,25,9,1..., dimensions={0} | all-to-all | bytes 2097152 | tf_op jit(solution)/shard_map/all_to_all | solution.py:323
  33.8 2.7 %dips.1 = f32[32,64,128]{2,1,0:T(8,128)} custom-call(f32[128,16,128]{2,1,0:T(8,128)S(1)} %bitcast.8), custom_call_target="tpu_custom_call" | custom-call | tf_op jit(solution)/shard_map/dips/pallas_call | solution.py:327
